TPU v7x, 1024 devices: a whole 4x4x32 slice. The times are simulated.
1024 devices in a mesh: gx: 32 (over z), gy: 4 (over y), gz: 8 (over x, core).
Axes of the slice: x: 4, y: 4, z: 32, core: 2. Of those that a mesh axis runs over, the one named last changes fastest.
Arguments:
- bands: bfloat16 [64, 128, 64, 1024], P(None, 'gx', 'gy', 'gz'), may hold values from -48 to 48
- potential: float32 [128, 64, 1024], P('gx', 'gy', 'gz'), may hold values from -3 to 0
- coupling: float32 [2048], replicated, may hold values from 0.5 to 2
- proj_atom: int32 [1024, 256], P(('gx', 'gy', 'gz')), may hold values from 0 to 2047, as said below
- proj_cell: int32 [1024, 256], P(('gx', 'gy', 'gz')), may hold values from 0 to 8191
- proj_value: float32 [1024, 256], P(('gx', 'gy', 'gz')), may hold values from -1 to 1
Outputs:
- filtered: bfloat16 [64, 128, 64, 1024], P(None, 'gx', 'gy', 'gz')
- gram: float32 [64, 64], replicated
Inputs may be any that keep to these rules, and one draw needn't show every extreme that they name: `proj_atom`: every point listed in row d names an atom whose owning device block differs from d's block by at most one along each of gx, gy and gz.
All inputs are finite; a program needn't handle non-finite values.
Results may differ from a plain program's by a relative error of at most 0.00065.
The roundings to bfloat16 on the way count: a program that leaves them out, or rounds other values in their place, can miss the bound.
Values may be sent and summed in bfloat16 or wider, within the bound.
A program may use at most 64 MiB of HBM per device.

v0:
```python
import jax
import jax.numpy as jnp
from jax import lax
from jax.sharding import PartitionSpec as P

A_DEV = 2
DEGREE = 3


STENCIL = (-205.0 / 72.0, 8.0 / 5.0, -1.0 / 5.0, 8.0 / 315.0, -1.0 / 560.0)
FILTER_CENTRE = 8.25
FILTER_HALF = 7.75


def with_halo(block, sides, width):
    for axis, dim in sides:
        count = lax.axis_size(axis)
        forward = [(i, i + 1) for i in range(count - 1)]
        backward = [(target, source) for source, target in forward]
        low = lax.ppermute(
            lax.slice_in_dim(block, block.shape[dim] - width, None, axis=dim), axis, forward
        )
        high = lax.ppermute(lax.slice_in_dim(block, 0, width, axis=dim), axis, backward)
        block = jnp.concatenate([low, block, high], axis=dim)
    return block


def axis_term(extended, dim, length):
    total = jnp.zeros_like(lax.slice_in_dim(extended, 4, 4 + length, axis=dim)).astype(jnp.float32)
    for offset in range(1, 5):
        upper = lax.slice_in_dim(extended, 4 + offset, 4 + offset + length, axis=dim).astype(
            jnp.float32
        )
        lower = lax.slice_in_dim(extended, 4 - offset, 4 - offset + length, axis=dim).astype(
            jnp.float32
        )
        total = total + STENCIL[offset] * (upper + lower)
    return total


def shards(bands, potential, coupling, proj_atom, proj_cell, proj_value):
    count, size_x, size_y, size_z = bands.shape
    cells_dev = size_x * size_y * size_z
    atoms = proj_atom[0]
    cells = proj_cell[0]
    values = proj_value[0]
    span_y = lax.axis_size("gy")
    span_z = lax.axis_size("gz")
    devices = lax.axis_size("gx") * span_y * span_z
    here_x = lax.axis_index("gx")
    here_y = lax.axis_index("gy")
    here_z = lax.axis_index("gz")
    owners = atoms // A_DEV
    slots = atoms % A_DEV
    keys = (
        ((owners // (span_y * span_z) - here_x + 1) * 3 + owners // span_z % span_y - here_y + 1)
        * 3
        + owners % span_z
        - here_z
        + 1
    ) * A_DEV + slots
    linear = (here_x * span_y + here_y) * span_z + here_z
    own_coupling = lax.dynamic_slice_in_dim(coupling, linear * A_DEV, A_DEV)

    def projector(flat):
        picked = flat[:, cells] * values[None, :]
        partial_value = jax.ops.segment_sum(picked.T, keys, num_segments=27 * A_DEV).reshape(
            3, 3, 3, A_DEV, count
        )
        arrived = with_halo(partial_value, (("gx", 0), ("gy", 1), ("gz", 2)), 1)
        totals = jnp.sum(arrived[0::2, 0::2, 0::2], axis=(0, 1, 2))
        scaled = totals * own_coupling[:, None]
        table = with_halo(scaled[None, None, None], (("gx", 0), ("gy", 1), ("gz", 2)), 1)
        back = table.reshape(27 * A_DEV, count)[keys]
        return jnp.zeros_like(flat).at[:, cells].add((back * values[:, None]).T)

    def apply_h(current):
        field = current.astype(jnp.float32)
        extended = with_halo(current, (("gx", 1), ("gy", 2), ("gz", 3)), 4)
        term_x = axis_term(extended[:, :, 4 : 4 + size_y, 4 : 4 + size_z], 1, size_x)
        term_y = axis_term(extended[:, 4 : 4 + size_x, :, 4 : 4 + size_z], 2, size_y)
        term_z = axis_term(extended[:, 4 : 4 + size_x, 4 : 4 + size_y, :], 3, size_z)
        lap = 3.0 * STENCIL[0] * field + term_x + term_y + term_z
        projected = projector(field.reshape(count, cells_dev)).reshape(field.shape)
        return -0.5 * lap + potential[None] * field + projected

    previous = bands
    image = apply_h(bands)
    current = ((image - FILTER_CENTRE * bands.astype(jnp.float32)) / FILTER_HALF).astype(
        jnp.bfloat16
    )
    for step in range(DEGREE - 1):
        image = apply_h(current)
        following = 2.0 * (
            image - FILTER_CENTRE * current.astype(jnp.float32)
        ) / FILTER_HALF - previous.astype(jnp.float32)
        previous = current
        current = following.astype(jnp.bfloat16)
    flat_out = current.reshape(count, cells_dev)
    local_gram = jnp.dot(flat_out, flat_out.T, preferred_element_type=jnp.float32)
    gram = lax.psum(local_gram, ("gx", "gy", "gz")) / float(cells_dev * devices)
    return (current, gram)


def solution(mesh):
    in_specs = (
        P(None, "gx", "gy", "gz"),
        P("gx", "gy", "gz"),
        P(),
        P(("gx", "gy", "gz"), None),
        P(("gx", "gy", "gz"), None),
        P(("gx", "gy", "gz"), None),
    )
    out_specs = (P(None, "gx", "gy", "gz"), P())
    return jax.shard_map(shards, mesh=mesh, in_specs=in_specs, out_specs=out_specs, check_vma=False)
```

profile of v0, /device:TPU:1, one launch (start us, length us, event | category | flops | bytes accessed | tf_op | source)
XLA Modules:
  0.0 619.7 jit_solution(12914222940975147024)
XLA Ops:
  9.5 10.6 %collective-permute-done.1 = bf16[64,4,16,128]{3,0,2,1:T(8,128)(2,1)S(1)} collective-permute-done((bf16[64,4,16,128]{3,0,2,1:T(8,128)(2,1)}, bf16[64,4,16,128]{3,0,2,1:T(8,128)(2,1)S(1)}, u32[]{:S(2)}, u32[]{:S(2)}) %collective-permute-start.1) | collective-permute-done | bytes 1048608 | tf_op jit(solution)/shard_map/ppermute | solution.py:20
  32.2 13.6 %collective-permute-start.6 = (f32[1,3,3,2,64]{4,3,2,1,0:T(2,128)S(1)}, f32[1,3,3,2,64]{4,3,2,1,0:T(2,128)S(1)}, u32[]{:S(2)}, u32[]{:S(2)}) collective-permute-start(f32[1,3,3,2,64]{4,3,2,1,0:T(2,128)S(1)} %slice.462), channel_id=1, source_target_pairs={{0,32},{32,64},{64,96},{96,128},{128,160},{160,192},{192,224},{224... | collective-permute-start | bytes 13832 | tf_op jit(solution)/shard_map/ppermute | solution.py:20
  59.5 5.5 collective-permute-start.3
  65.0 6.6 %collective-permute-start.10 = (f32[5,5,1,2,64]{4,3,2,1,0:T(2,128)S(1)}, f32[5,5,1,2,64]{4,3,2,1,0:T(2,128)S(1)}, u32[]{:S(2)}, u32[]{:S(2)}) collective-permute-start(f32[5,5,1,2,64]{4,3,2,1,0:T(2,128)S(1)} %get-tuple-element.36), channel_id=1, source_target_pairs={{0,1},{1,2},{2,3},{3,4},{4,5},{5,6},{6,7},{8,9},{9,10},{10,11},{11... | collective-permute-start | bytes 38408 | tf_op jit(solution)/shard_map/ppermute | solution.py:20
  98.4 6.1 fusion.51
  133.5 23.8 %multiply_convert_fusion = bf16[64,4,16,128]{3,0,2,1:T(8,128)(2,1)S(1)} fusion(f32[64,4,16,128]{3,0,2,1:T(8,128)} %copy.60, bf16[64,4,16,128]{3,0,2,1:T(8,128)(2,1)S(1)} %collective-permute-done.1, bf16[64,4,16,128]{3,0,2,1:T(8,128)(2,1)} %copy-done.2, bf16[64,12,16,128]{3,0,2,1:T(8,128)(2,1)} %get-tuple-element.25, ...), kind=kLoop, calls=%fused_computation.49 | loop fusion | flops 78643200 | bytes 17629184 | tf_op jit(solution)/shard_map/convert_element_type | solution.py:89
  157.2 5.3 collective-permute-start.19
  169.6 5.4 collective-permute-start.24
  176.3 9.2 %collective-permute-done.24 = f32[1,3,3,2,64]{4,3,2,1,0:T(2,128)S(1)} collective-permute-done((f32[1,3,3,2,64]{4,3,2,1,0:T(2,128)S(1)}, f32[1,3,3,2,64]{4,3,2,1,0:T(2,128)S(1)}, u32[]{:S(2)}, u32[]{:S(2)}) %collective-permute-start.24) | collective-permute-done | bytes 4640 | tf_op jit(solution)/shard_map/ppermute | solution.py:20
  185.5 5.4 collective-permute-done.25
  199.3 5.1 collective-permute-start.28
  214.4 5.5 collective-permute-start.30
  233.1 5.3 collective-permute-start.34
  249.6 6.1 fusion.50
  287.1 16.5 %subtract_convert_fusion.1 = bf16[64,4,16,128]{3,0,2,1:T(8,128)(2,1)S(1)} fusion(f32[64,4,16,128]{3,0,2,1:T(8,128)} %copy.66, bf16[64,4,16,128]{3,0,2,1:T(8,128)(2,1)S(1)} %collective-permute-done.19, bf16[64,4,16,128]{3,0,2,1:T(8,128)(2,1)} %copy-done, bf16[64,4,16,128]{3,0,2,1:T(8,128)(2,1)S(1)} %multiply_convert_fusion, bf16[64,12,24,4]{3,0,2,1:T(8,128)(2,1)} %copy.64, ...), kind=kLoop, calls=%fused_computation.48 | loop fusion | flops 93323264 | bytes 17629184 | tf_op jit(solution)/shard_map/convert_element_type | solution.py:98
  315.6 5.7 collective-permute-start.42
  322.7 6.1 collective-permute-done.42
  328.8 5.6 collective-permute-done.43
  341.2 7.0 %collective-permute-start.46 = (f32[5,5,1,2,64]{4,3,2,1,0:T(2,128)S(1)}, f32[5,5,1,2,64]{4,3,2,1,0:T(2,128)S(1)}, u32[]{:S(2)}, u32[]{:S(2)}) collective-permute-start(f32[5,5,1,2,64]{4,3,2,1,0:T(2,128)S(1)} %get-tuple-element.32), channel_id=1, source_target_pairs={{0,1},{1,2},{2,3},{3,4},{4,5},{5,6},{6,7},{8,9},{9,10},{10,11},{11... | collective-permute-start | bytes 38408 | tf_op jit(solution)/shard_map/ppermute | solution.py:20
  358.5 5.1 collective-permute-start.48
  374.3 7.6 %collective-permute-start.52 = (f32[3,3,1,2,64]{4,3,2,1,0:T(2,128)S(1)}, f32[3,3,1,2,64]{4,3,2,1,0:T(2,128)S(1)}, u32[]{:S(2)}, u32[]{:S(2)}) collective-permute-start(f32[3,3,1,2,64]{4,3,2,1,0:T(2,128)S(1)} %pad_maximum_fusion.60), channel_id=1, source_target_pairs={{0,1},{1,2},{2,3},{3,4},{4,5},{5,6},{6,7},{8,9},{9,10},{10,11},{11... | collective-permute-start | bytes 13832 | tf_op jit(solution)/shard_map/ppermute | solution.py:20
  395.0 6.1 fusion.49
  432.5 16.1 %subtract_convert_fusion = bf16[64,4,16,128]{3,0,2,1:T(8,128)(2,1)S(1)} fusion(f32[64,4,16,128]{3,0,2,1:T(8,128)} %copy.72, bf16[64,4,16,128]{3,0,2,1:T(8,128)(2,1)S(1)} %collective-permute-done.37, bf16[64,4,16,128]{3,0,2,1:T(8,128)(2,1)} %collective-permute-done.36, bf16[64,4,16,128]{3,0,2,1:T(8,128)(2,1)S(1)} %subtract_convert_fusion.1, ...), kind=kLoop, calls=%fused_computation.47 | loop fusion | flops 93323264 | bytes 17629184 | tf_op jit(solution)/shard_map/convert_element_type | solution.py:98
  450.6 168.2 %psum.7 = f32[64,64]{1,0:T(8,128)S(1)} all-reduce(f32[64,64]{1,0:T(8,128)S(1)} %convolution_bitcast_fusion), channel_id=1, replica_groups=mesh['gx'=32,'gy'=4,'gz'=8] {'gx','gy','gz'}, use_global_device_ids=true, to_apply=%region_9.10 | all-reduce | flops 4096 | bytes 32768 | tf_op jit(solution)/shard_map/psum | solution.py:101
  (199 shorter events, 260.5 us)
Async XLA Ops:
  3.5 16.5 %collective-permute-start.1 = (bf16[64,4,16,128]{3,0,2,1:T(8,128)(2,1)}, bf16[64,4,16,128]{3,0,2,1:T(8,128)(2,1)S(1)}, u32[]{:S(2)}, u32[]{:S(2)}) collective-permute-start(bf16[64,4,16,128]{3,0,2,1:T(8,128)(2,1)} %copy.49), channel_id=1, source_target_pairs={{0,32},{32,64},{64,96},{96,128},{128,160},{160,192},{192,224},{224... | collective-permute-start | bytes 3145736 | tf_op jit(solution)/shard_map/ppermute | solution.py:20
  8.1 39.1 %collective-permute-start = (bf16[64,4,16,128]{3,0,2,1:T(8,128)(2,1)}, bf16[64,4,16,128]{3,0,2,1:T(8,128)(2,1)S(1)}, u32[]{:S(2)}, u32[]{:S(2)}) collective-permute-start(bf16[64,4,16,128]{3,0,2,1:T(8,128)(2,1)} %copy.49), channel_id=1, source_target_pairs={{32,0},{64,32},{96,64},{128,96},{160,128},{192,160},{224,192},{256... | collective-permute-start | bytes 3145736 | tf_op jit(solution)/shard_map/ppermute | solution.py:23
  32.2 17.1 %collective-permute-start.6 = (f32[1,3,3,2,64]{4,3,2,1,0:T(2,128)S(1)}, f32[1,3,3,2,64]{4,3,2,1,0:T(2,128)S(1)}, u32[]{:S(2)}, u32[]{:S(2)}) collective-permute-start(f32[1,3,3,2,64]{4,3,2,1,0:T(2,128)S(1)} %slice.462), channel_id=1, source_target_pairs={{0,32},{32,64},{64,96},{96,128},{128,160},{160,192},{192,224},{224... | collective-permute-start | bytes 13832 | tf_op jit(solution)/shard_map/ppermute | solution.py:20
  50.9 14.0 %collective-permute-start.8 = (f32[5,1,3,2,64]{4,3,2,1,0:T(2,128)S(1)}, f32[5,1,3,2,64]{4,3,2,1,0:T(2,128)S(1)}, u32[]{:S(2)}, u32[]{:S(2)}) collective-permute-start(f32[5,1,3,2,64]{4,3,2,1,0:T(2,128)S(1)} %get-tuple-element.42), channel_id=1, source_target_pairs={{0,8},{8,16},{16,24},{1,9},{9,17},{17,25},{2,10},{10,18},{18,26},{... | collective-permute-start | bytes 23048 | tf_op jit(solution)/shard_map/ppermute | solution.py:20
  58.2 37.5 %collective-permute-start.2 = (bf16[64,12,4,128]{3,0,2,1:T(8,128)(2,1)}, bf16[64,12,4,128]{3,0,2,1:T(8,128)(2,1)S(1)}, u32[]{:S(2)}, u32[]{:S(2)}) collective-permute-start(bf16[64,12,4,128]{3,0,2,1:T(8,128)(2,1)} %get-tuple-element.22), channel_id=1, source_target_pairs={{8,0},{16,8},{24,16},{9,1},{17,9},{25,17},{10,2},{18,10},{26,18},{... | collective-permute-start | bytes 2359304 | tf_op jit(solution)/shard_map/ppermute | solution.py:23
  59.5 36.3 %collective-permute-start.3 = (bf16[64,12,4,128]{3,0,2,1:T(8,128)(2,1)}, bf16[64,12,4,128]{3,0,2,1:T(8,128)(2,1)}, u32[]{:S(2)}, u32[]{:S(2)}) collective-permute-start(bf16[64,12,4,128]{3,0,2,1:T(8,128)(2,1)} %get-tuple-element.23), channel_id=1, source_target_pairs={{0,8},{8,16},{16,24},{1,9},{9,17},{17,25},{2,10},{10,18},{18,26},{... | collective-permute-start | bytes 2359304 | tf_op jit(solution)/shard_map/ppermute | solution.py:20
  90.1 27.1 %collective-permute-start.17 = (f32[3,3,1,2,64]{4,3,2,1,0:T(2,128)S(1)}, f32[3,3,1,2,64]{4,3,2,1,0:T(2,128)S(1)}, u32[]{:S(2)}, u32[]{:S(2)}) collective-permute-start(f32[3,3,1,2,64]{4,3,2,1,0:T(2,128)S(1)} %pad_maximum_fusion.58), channel_id=1, source_target_pairs={{1,0},{2,1},{3,2},{4,3},{5,4},{6,5},{7,6},{9,8},{10,9},{11,10},{12... | collective-permute-start | bytes 13832 | tf_op jit(solution)/shard_map/ppermute | solution.py:23
  92.1 25.2 %collective-permute-start.16 = (f32[3,3,1,2,64]{4,3,2,1,0:T(2,128)S(1)}, f32[3,3,1,2,64]{4,3,2,1,0:T(2,128)S(1)}, u32[]{:S(2)}, u32[]{:S(2)}) collective-permute-start(f32[3,3,1,2,64]{4,3,2,1,0:T(2,128)S(1)} %pad_maximum_fusion.58), channel_id=1, source_target_pairs={{0,1},{1,2},{2,3},{3,4},{4,5},{5,6},{6,7},{8,9},{9,10},{10,11},{11... | collective-permute-start | bytes 13832 | tf_op jit(solution)/shard_map/ppermute | solution.py:20
  112.8 16.9 %collective-permute-start.5 = (bf16[64,12,24,4]{0,2,3,1:T(8,128)(2,1)S(1)}, bf16[64,12,24,4]{0,2,3,1:T(8,128)(2,1)S(1)}, u32[]{:S(2)}, u32[]{:S(2)}) collective-permute-start(bf16[64,12,24,4]{0,2,3,1:T(8,128)(2,1)S(1)} %copy.57), channel_id=1, source_target_pairs={{0,1},{1,2},{2,3},{3,4},{4,5},{5,6},{6,7},{8,9},{9,10},{10,11},{11... | collective-permute-start | bytes 442376 | tf_op jit(solution)/shard_map/ppermute | solution.py:20
  157.2 49.2 %collective-permute-start.19 = (bf16[64,4,16,128]{3,0,2,1:T(8,128)(2,1)S(1)}, bf16[64,4,16,128]{3,0,2,1:T(8,128)(2,1)S(1)}, u32[]{:S(2)}, u32[]{:S(2)}) collective-permute-start(bf16[64,4,16,128]{3,0,2,1:T(8,128)(2,1)S(1)} %multiply_convert_fusion), channel_id=1, source_target_pairs={{0,32},{32,64},{64,96},{96,128},{128,160},{160,192},{192,224},{224... | collective-permute-start | bytes 3145736 | tf_op jit(solution)/shard_map/ppermute | solution.py:20
  162.5 43.9 %collective-permute-start.18 = (bf16[64,4,16,128]{3,0,2,1:T(8,128)(2,1)S(1)}, bf16[64,4,16,128]{3,0,2,1:T(8,128)(2,1)S(1)}, u32[]{:S(2)}, u32[]{:S(2)}) collective-permute-start(bf16[64,4,16,128]{3,0,2,1:T(8,128)(2,1)S(1)} %multiply_convert_fusion), channel_id=1, source_target_pairs={{32,0},{64,32},{96,64},{128,96},{160,128},{192,160},{224,192},{256... | collective-permute-start | bytes 3145736 | tf_op jit(solution)/shard_map/ppermute | solution.py:23
  169.6 15.9 %collective-permute-start.24 = (f32[1,3,3,2,64]{4,3,2,1,0:T(2,128)S(1)}, f32[1,3,3,2,64]{4,3,2,1,0:T(2,128)S(1)}, u32[]{:S(2)}, u32[]{:S(2)}) collective-permute-start(f32[1,3,3,2,64]{4,3,2,1,0:T(2,128)S(1)} %slice.497), channel_id=1, source_target_pairs={{0,32},{32,64},{64,96},{96,128},{128,160},{160,192},{192,224},{224... | collective-permute-start | bytes 13832 | tf_op jit(solution)/shard_map/ppermute | solution.py:20
  175.0 15.9 %collective-permute-start.25 = (f32[1,3,3,2,64]{4,3,2,1,0:T(2,128)S(1)}, f32[1,3,3,2,64]{4,3,2,1,0:T(2,128)S(1)}, u32[]{:S(2)}, u32[]{:S(2)}) collective-permute-start(f32[1,3,3,2,64]{4,3,2,1,0:T(2,128)S(1)} %slice.499), channel_id=1, source_target_pairs={{32,0},{64,32},{96,64},{128,96},{160,128},{192,160},{224,192},{256... | collective-permute-start | bytes 13832 | tf_op jit(solution)/shard_map/ppermute | solution.py:23
  199.3 13.5 %collective-permute-start.28 = (f32[5,5,1,2,64]{4,3,2,1,0:T(2,128)S(1)}, f32[5,5,1,2,64]{4,3,2,1,0:T(2,128)S(1)}, u32[]{:S(2)}, u32[]{:S(2)}) collective-permute-start(f32[5,5,1,2,64]{4,3,2,1,0:T(2,128)S(1)} %get-tuple-element.34), channel_id=1, source_target_pairs={{0,1},{1,2},{2,3},{3,4},{4,5},{5,6},{6,7},{8,9},{9,10},{10,11},{11... | collective-permute-start | bytes 38408 | tf_op jit(solution)/shard_map/ppermute | solution.py:20
  207.9 39.9 %collective-permute-start.21 = (bf16[64,12,4,128]{3,0,2,1:T(8,128)(2,1)}, bf16[64,12,4,128]{3,0,2,1:T(8,128)(2,1)}, u32[]{:S(2)}, u32[]{:S(2)}) collective-permute-start(bf16[64,12,4,128]{3,0,2,1:T(8,128)(2,1)} %get-tuple-element.20), channel_id=1, source_target_pairs={{0,8},{8,16},{16,24},{1,9},{9,17},{17,25},{2,10},{10,18},{18,26},{... | collective-permute-start | bytes 2359304 | tf_op jit(solution)/shard_map/ppermute | solution.py:20
  211.6 36.2 %collective-permute-start.20 = (bf16[64,12,4,128]{3,0,2,1:T(8,128)(2,1)}, bf16[64,12,4,128]{3,0,2,1:T(8,128)(2,1)}, u32[]{:S(2)}, u32[]{:S(2)}) collective-permute-start(bf16[64,12,4,128]{3,0,2,1:T(8,128)(2,1)} %get-tuple-element.21), channel_id=1, source_target_pairs={{8,0},{16,8},{24,16},{9,1},{17,9},{25,17},{10,2},{18,10},{26,18},{... | collective-permute-start | bytes 2359304 | tf_op jit(solution)/shard_map/ppermute | solution.py:23
  264.8 17.5 %collective-permute-start.23 = (bf16[64,12,24,4]{0,2,3,1:T(8,128)(2,1)S(1)}, bf16[64,12,24,4]{0,2,3,1:T(8,128)(2,1)}, u32[]{:S(2)}, u32[]{:S(2)}) collective-permute-start(bf16[64,12,24,4]{0,2,3,1:T(8,128)(2,1)S(1)} %copy.63), channel_id=1, source_target_pairs={{0,1},{1,2},{2,3},{3,4},{4,5},{5,6},{6,7},{8,9},{9,10},{10,11},{11... | collective-permute-start | bytes 442376 | tf_op jit(solution)/shard_map/ppermute | solution.py:20
  303.7 46.5 %collective-permute-start.37 = (bf16[64,4,16,128]{3,0,2,1:T(8,128)(2,1)S(1)}, bf16[64,4,16,128]{3,0,2,1:T(8,128)(2,1)S(1)}, u32[]{:S(2)}, u32[]{:S(2)}) collective-permute-start(bf16[64,4,16,128]{3,0,2,1:T(8,128)(2,1)S(1)} %subtract_convert_fusion.1), channel_id=1, source_target_pairs={{0,32},{32,64},{64,96},{96,128},{128,160},{160,192},{192,224},{224... | collective-permute-start | bytes 3145736 | tf_op jit(solution)/shard_map/ppermute | solution.py:20
  308.6 41.5 %collective-permute-start.36 = (bf16[64,4,16,128]{3,0,2,1:T(8,128)(2,1)S(1)}, bf16[64,4,16,128]{3,0,2,1:T(8,128)(2,1)}, u32[]{:S(2)}, u32[]{:S(2)}) collective-permute-start(bf16[64,4,16,128]{3,0,2,1:T(8,128)(2,1)S(1)} %subtract_convert_fusion.1), channel_id=1, source_target_pairs={{32,0},{64,32},{96,64},{128,96},{160,128},{192,160},{224,192},{256... | collective-permute-start | bytes 3145736 | tf_op jit(solution)/shard_map/ppermute | solution.py:23
  315.6 13.1 %collective-permute-start.42 = (f32[1,3,3,2,64]{4,3,2,1,0:T(2,128)S(1)}, f32[1,3,3,2,64]{4,3,2,1,0:T(2,128)S(1)}, u32[]{:S(2)}, u32[]{:S(2)}) collective-permute-start(f32[1,3,3,2,64]{4,3,2,1,0:T(2,128)S(1)} %slice.532), channel_id=1, source_target_pairs={{0,32},{32,64},{64,96},{96,128},{128,160},{160,192},{192,224},{224... | collective-permute-start | bytes 13832 | tf_op jit(solution)/shard_map/ppermute | solution.py:20
  341.2 15.8 %collective-permute-start.46 = (f32[5,5,1,2,64]{4,3,2,1,0:T(2,128)S(1)}, f32[5,5,1,2,64]{4,3,2,1,0:T(2,128)S(1)}, u32[]{:S(2)}, u32[]{:S(2)}) collective-permute-start(f32[5,5,1,2,64]{4,3,2,1,0:T(2,128)S(1)} %get-tuple-element.32), channel_id=1, source_target_pairs={{0,1},{1,2},{2,3},{3,4},{4,5},{5,6},{6,7},{8,9},{9,10},{10,11},{11... | collective-permute-start | bytes 38408 | tf_op jit(solution)/shard_map/ppermute | solution.py:20
  352.5 38.5 %collective-permute-start.39 = (bf16[64,12,4,128]{3,0,2,1:T(8,128)(2,1)}, bf16[64,12,4,128]{3,0,2,1:T(8,128)(2,1)}, u32[]{:S(2)}, u32[]{:S(2)}) collective-permute-start(bf16[64,12,4,128]{3,0,2,1:T(8,128)(2,1)} %get-tuple-element.16), channel_id=1, source_target_pairs={{0,8},{8,16},{16,24},{1,9},{9,17},{17,25},{2,10},{10,18},{18,26},{... | collective-permute-start | bytes 2359304 | tf_op jit(solution)/shard_map/ppermute | solution.py:20
  355.7 35.2 %collective-permute-start.38 = (bf16[64,12,4,128]{3,0,2,1:T(8,128)(2,1)}, bf16[64,12,4,128]{3,0,2,1:T(8,128)(2,1)}, u32[]{:S(2)}, u32[]{:S(2)}) collective-permute-start(bf16[64,12,4,128]{3,0,2,1:T(8,128)(2,1)} %get-tuple-element.17), channel_id=1, source_target_pairs={{8,0},{16,8},{24,16},{9,1},{17,9},{25,17},{10,2},{18,10},{26,18},{... | collective-permute-start | bytes 2359304 | tf_op jit(solution)/shard_map/ppermute | solution.py:23
  410.2 17.5 %collective-permute-start.41 = (bf16[64,12,24,4]{0,2,3,1:T(8,128)(2,1)S(1)}, bf16[64,12,24,4]{0,2,3,1:T(8,128)(2,1)}, u32[]{:S(2)}, u32[]{:S(2)}) collective-permute-start(bf16[64,12,24,4]{0,2,3,1:T(8,128)(2,1)S(1)} %copy.69), channel_id=1, source_target_pairs={{0,1},{1,2},{2,3},{3,4},{4,5},{5,6},{6,7},{8,9},{9,10},{10,11},{11... | collective-permute-start | bytes 442376 | tf_op jit(solution)/shard_map/ppermute | solution.py:20
  (38 other events, 340.8 us)
where the time goes:
time: 631 us; the launch traced here: 620 us
  starting transfers between devices  177 us (28%)
  blocking collectives  168 us (27%)
  other arithmetic  107 us (17%)
  local copies, waits for them, and re-layouts  104 us (16%)
  waiting for transfers between devices  61.4 us (10%)
    psum x1, blocking collectives, shards(): gram = lax.psum(local_gram, ('gx', 'gy', 'gz')) / float(cells_dev * devices)  168 us
    ppermute x27, starting transfers between devices, with_halo(): lax.ppermute(lax.slice_in_dim(block, block.shape[dim] - width, None, axis...  136 us
    ppermute x27, starting transfers between devices, with_halo(): lax.ppermute(lax.slice_in_dim(block, 0, width, axis=dim), axis, backward)  40.5 us
    slice x13, local copies, waits for them, and re-layouts, with_halo(): lax.slice_in_dim(block, 0, width, axis=dim)  35 us
    convert_element_type x2, other arithmetic, shards(): current = following.astype(jnp.bfloat16)  32.6 us
    ppermute x27, waiting for transfers between devices, with_halo(): lax.ppermute(lax.slice_in_dim(block, 0, width, axis=dim), axis, backward)  31.4 us
    ppermute x27, waiting for transfers between devices, with_halo(): lax.ppermute(lax.slice_in_dim(block, block.shape[dim] - width, None, axis...  30 us
    convert_element_type x1, other arithmetic, shards(): ((image - FILTER_CENTRE * bands.astype(jnp.float32)) / FILTER_HALF).astyp...  23.8 us
  transfers between devices with their start and end apart: 54, of which 19 were waited for; matrix products, arithmetic and copies ran while one was open for 16% of the time, Pallas kernels for 0%

commit v1 on v0

v1 whole, which is shorter than its diff:
```python
import jax
import jax.numpy as jnp
import ml_dtypes
import numpy as np
from jax import lax
from jax.experimental import pallas as pl
from jax.experimental.pallas import tpu as pltpu
from jax.sharding import PartitionSpec as P

A_DEV = 2
DEGREE = 3
STENCIL = (-205.0 / 72.0, 8.0 / 5.0, -1.0 / 5.0, 8.0 / 315.0, -1.0 / 560.0)
FILTER_CENTRE = 8.25
FILTER_HALF = 7.75

GROUP = 16
KEYS = 64
SPAN = {}
STAGES = (("gz", 2), ("gy", 6), ("gx", 18), ("gx", 18), ("gy", 6), ("gz", 2))
OWN_LANE = 26
F32 = jnp.float32
BF16 = jnp.bfloat16


def beside(axis, offset):
    n = SPAN[axis]
    return {axis: lax.rem(lax.axis_index(axis) + offset + n, n)}


def split(value):
    high = value.astype(BF16)
    return high, (value - high.astype(F32)).astype(BF16)


def kernel(
    y0_ref, pot_ref, coup_ref, atom_ref, cell_ref, val_ref, wz_ref,
    out_ref, gram_ref,
    field, y_halo, z_pack, z_halo, gather_op, scatter_op, key_in, key_out, table, coup_row, potq,
    q_send, q_recv, q0_send, q0_recv,
    g_part, r_z, s_z, r_y, s_y, r_x, g_all,
    load_sem, out_sem, x_ss, x_rs, y_ss, y_rs, z_ss, z_rs, q_ss, q_rs, q0_ss, q0_rs,
    sz, rz, sy, ry, sx, rx,
):
    groups, size_x, size_y = field.shape[1], 4, field.shape[3]
    span_x, span_y, span_z = SPAN["gx"], SPAN["gy"], SPAN["gz"]
    here = {axis: lax.axis_index(axis) for axis in SPAN}
    first = {a: jnp.where(here[a] == 0, 0.0, 1.0).astype(F32) for a in SPAN}
    last = {a: jnp.where(here[a] == SPAN[a] - 1, 0.0, 1.0).astype(F32) for a in SPAN}

    def load_copy(g):
        return pltpu.make_async_copy(y0_ref.at[g], field.at[0, g, pl.ds(4, 4)], load_sem.at[g])

    def out_copy(g):
        return pltpu.make_async_copy(
            field.at[DEGREE, g, pl.ds(4, 4)], out_ref.at[g], out_sem.at[g]
        )

    def x_copy(k, g, x, side):
        return pltpu.make_async_remote_copy(
            field.at[k, g, 4 + x],
            field.at[k, g, x if side == 0 else 8 + x],
            x_ss.at[k, g, x, side],
            x_rs.at[k, g, x, side],
            device_id=beside("gx", 1 - 2 * side),
        )

    def y_copy(k, g, side):
        rows = pl.ds(12, 4) if side == 0 else pl.ds(0, 4)
        return pltpu.make_async_remote_copy(
            field.at[k, g, pl.ds(4, 4), rows],
            y_halo.at[k, g, side],
            y_ss.at[k, g, side],
            y_rs.at[k, g, side],
            device_id=beside("gy", 1 - 2 * side),
        )

    def z_copy(k, g, side):
        return pltpu.make_async_remote_copy(
            z_pack.at[k, g],
            z_halo.at[k, g, side],
            z_ss.at[k, g, side],
            z_rs.at[k, g, side],
            device_id=beside("gz", 1 - 2 * side),
        )

    def q_copy(chain, stage, side):
        return pltpu.make_async_remote_copy(
            q_send.at[chain, stage],
            q_recv.at[chain, stage, side],
            q_ss.at[chain, stage, side],
            q_rs.at[chain, stage, side],
            device_id=beside(STAGES[stage][0], 1 - 2 * side),
        )

    def q0_copy(stage, side):
        return pltpu.make_async_remote_copy(
            q0_send.at[stage],
            q0_recv.at[stage, side],
            q0_ss.at[stage, side],
            q0_rs.at[stage, side],
            device_id=beside(STAGES[stage][0], 1 - 2 * side),
        )

    for g in range(groups):
        load_copy(g).start()
    barrier = pltpu.get_barrier_semaphore()
    partners = [(a, d) for a in ("gx", "gy", "gz") for d in (1, -1)]
    greeted = []
    for axis, offset in partners:
        greeted.append(beside(axis, offset))
    for d in range(2, span_z - 1):
        greeted.append(beside("gz", d))
    for d in range(2, span_y - 1):
        greeted.append(beside("gy", d))
    for d in range(2, span_x - 1):
        greeted.append(beside("gx", d))
    with jax.named_scope("entry"):
        for device in greeted:
            pl.semaphore_signal(barrier, 1, device_id=device)
        pl.semaphore_wait(barrier, len(greeted))

    lane = lax.broadcasted_iota(jnp.int32, (GROUP, 128), 1)
    low_half = lane < KEYS

    def pack_z(k, g, x, tiles):
        packed = jnp.zeros((GROUP, 128), F32)
        for y in range(size_y):
            moved = pltpu.roll(tiles[y], (8 * y + 4) % 128, 1)
            packed = jnp.where((lane >= 8 * y) & (lane < 8 * y + 8), moved, packed)
        z_pack[k, g, x] = packed.astype(BF16)

    def send_edges(k, g):
        for side in range(2):
            y_copy(k, g, side).start()
            z_copy(k, g, side).start()

    def gather(k, chosen):
        def one(x, acc):
            row = jnp.concatenate(
                [
                    jnp.concatenate([field[k, g, 4 + x, y] for y in range(size_y)], axis=1)
                    for g in chosen
                ],
                axis=0,
            )
            return acc + jnp.dot(row, gather_op[x], preferred_element_type=F32)

        none = jnp.zeros((GROUP * len(chosen), val_ref.shape[1]), F32)
        picked = lax.fori_loop(0, size_x, one, none)
        high, low = split(picked * val_ref[...])
        both = jnp.dot(high, key_in[...], preferred_element_type=F32)
        both = both + jnp.dot(low, key_in[...], preferred_element_type=F32)
        parts = [both[GROUP * i : GROUP * (i + 1)] for i in range(len(chosen))]
        return jnp.concatenate(
            [jnp.where(low_half[:8], part[:8], part[8:]) for part in parts], axis=0
        )

    def first_pump(pieces):
        for i in pieces:
            for side in range(2):
                x_copy(0, i // size_x, i % size_x, side).start()

    for g in range(groups):
        load_copy(g).wait()
        if g < 2:
            first_pump(range(size_x * g, size_x * (g + 1)))

    def first_pack(i, carry):
        g, x = lax.div(i, size_x), lax.rem(i, size_x)
        pack_z(0, g, x, [field[0, g, 4 + x, y].astype(F32) for y in range(size_y)])
        return carry

    with jax.named_scope("first_pack"):
        lax.fori_loop(0, groups * size_x, first_pack, 0)
        for g in range(groups):
            send_edges(0, g)

    atoms = atom_ref[...]
    bits_a, bits_y, bits_z = (n.bit_length() - 1 for n in (A_DEV, span_y, span_z))
    owner = atoms >> bits_a
    key = (
        (((owner >> (bits_y + bits_z)) - here["gx"] + 1) * 3
         + ((owner >> bits_z) & (span_y - 1)) - here["gy"] + 1) * 3
        + (owner & (span_z - 1)) - here["gz"] + 1
    ) * A_DEV + (atoms & (A_DEV - 1))
    entries = atoms.shape[1]
    key_rows = lax.broadcasted_iota(jnp.int32, (2 * KEYS, entries), 0)
    entry_key = jnp.where((key_rows & (KEYS - 1)) == key, 1.0, 0.0)
    key_out[...] = jnp.where(key_rows < KEYS, entry_key, 0.0).astype(BF16)
    key_in[...] = entry_key.T.astype(BF16)
    cells = cell_ref[...]
    z_rows = lax.broadcasted_iota(jnp.int32, (128, entries), 0)
    cell_rows = jnp.broadcast_to(cells.astype(F32), (128, entries)).T.astype(jnp.int32)
    z_lanes = lax.broadcasted_iota(jnp.int32, (entries, 128), 1)

    def build(r, carry):
        x, y = lax.div(r, size_y), lax.rem(r, size_y)
        hot = jnp.where(z_rows + r * 128 == cells, 1.0, 0.0).astype(BF16)
        gather_op[x, pl.ds(pl.multiple_of(y * 128, 128), 128)] = hot
        hot = jnp.where(z_lanes + r * 128 == cell_rows, 1.0, 0.0).astype(BF16)
        scatter_op[r] = hot
        return carry

    with jax.named_scope("build"):
        lax.fori_loop(0, size_x * size_y, build, 0)

    linear = (here["gx"] * SPAN["gy"] + here["gy"]) * SPAN["gz"] + here["gz"]
    row = coup_ref[pl.ds(lax.div(linear * A_DEV, 128), 1)]
    at = lax.rem(linear * A_DEV, 128)
    row = jnp.broadcast_to(row, (8, 128))
    lane8 = lane[:8]
    for half in range(2):
        shift = lax.rem(OWN_LANE + half * KEYS - at + 128, 128)
        moved = pltpu.roll(row, shift, 1)
        base = OWN_LANE + half * KEYS
        keep = (lane8 >= base) & (lane8 < base + A_DEV)
        part = jnp.where(keep, moved, 0.0) / FILTER_HALF
        coup_row[...] = part if half == 0 else coup_row[...] + part
    potq[...] = (pot_ref[...] - (FILTER_CENTRE + 1.5 * STENCIL[0])) / FILTER_HALF

    def combine(stage, own, from_low, from_high):
        shift = STAGES[stage][1]
        if stage < 3:
            total = own + pltpu.roll(from_low, 128 - shift, 1) + pltpu.roll(from_high, shift, 1)
            if stage == 2:
                scale = coup_row[...]
                total = total * jnp.concatenate([scale] * (own.shape[0] // 8), axis=0)
            return total
        return own + pltpu.roll(from_low, 128 - shift, 1) + pltpu.roll(from_high, shift, 1)

    def write_table(k, g, packed):
        turned = pltpu.roll(packed, KEYS, 1)
        first_bands = jnp.where(low_half[:8], packed, turned)
        other_bands = jnp.where(low_half[:8], turned, packed)
        whole = jnp.concatenate([first_bands, other_bands], axis=0)
        high, low = split(whole)
        back = jnp.dot(high, key_out[...], preferred_element_type=F32)
        back = back + jnp.dot(low, key_out[...], preferred_element_type=F32)
        back = back * val_ref[...]
        high = back.astype(BF16).astype(F32)
        table[k, g] = jnp.concatenate([high, back - high], axis=0).astype(BF16)

    def advance(chain, stage):
        for side in range(2):
            q_copy(chain, stage, side).wait()
        result = combine(
            stage, q_send[chain, stage], q_recv[chain, stage, 0], q_recv[chain, stage, 1]
        )
        if stage < 5:
            q_send[chain, stage + 1] = result
            for side in range(2):
                q_copy(chain, stage + 1, side).start()
        else:
            write_table(1 + lax.div(chain, groups), lax.rem(chain, groups), result)

    with jax.named_scope("first_exchange"):
        q0_send[0] = gather(0, range(groups))
        for stage in range(6):
            for side in range(2):
                q0_copy(stage, side).start()
            if stage == 2:
                first_pump(range(2 * size_x, 2 * size_x + 2))
            if stage == 3:
                first_pump(range(2 * size_x + 2, groups * size_x))
            for side in range(2):
                q0_copy(stage, side).wait()
            result = combine(stage, q0_send[stage], q0_recv[stage, 0], q0_recv[stage, 1])
            if stage < 5:
                q0_send[stage + 1] = result
            else:
                for g in range(groups):
                    write_table(0, g, result[8 * g : 8 * g + 8])

    stencil = [-0.5 * c / FILTER_HALF for c in STENCIL]

    def one_x(k, g, x):
        back = jnp.maximum(k - 1, 0)
        own = [field[k, g, 4 + x, y] for y in range(size_y)]
        ownf = [v.astype(F32) for v in own]
        low_y = [y_halo[k, g, 0, x, i].astype(F32) for i in range(4)]
        high_y = [y_halo[k, g, 1, x, i].astype(F32) for i in range(4)]
        line = low_y + ownf + high_y
        from_low = z_halo[k, g, 0, x].astype(F32) * first["gz"]
        from_high = z_halo[k, g, 1, x].astype(F32) * last["gz"]
        halo = jnp.where((lane & 7) < 4, from_low, from_high)
        turned = [halo if y == 0 else pltpu.roll(halo, 128 - 8 * y, 1) for y in range(size_y)]
        left = jnp.concatenate(
            [jnp.concatenate([own[y], turned[y].astype(BF16)], axis=1) for y in range(size_y)],
            axis=0,
        )
        z_term = jnp.dot(left, wz_ref[...], preferred_element_type=F32)
        scale = jnp.where(k == 0, 1.0, 2.0).astype(F32)
        keep = jnp.where(k == 0, 0.0, 1.0).astype(F32)
        c_low, c_high = [], []
        for m in range(1, 5):
            c_low.append(jnp.where(x - m >= 0, 1.0, first["gx"]) * stencil[m])
            c_high.append(jnp.where(x + m <= 3, 1.0, last["gx"]) * stencil[m])
        tiles = []
        coef = table[k, g]
        for y in range(size_y):
            total = ownf[y] * potq[x, pl.ds(y, 1)]
            for m in range(1, 5):
                total += c_low[m - 1] * field[k, g, 4 + x - m, y].astype(F32)
                total += c_high[m - 1] * field[k, g, 4 + x + m, y].astype(F32)
                under, over = line[4 + y - m], line[4 + y + m]
                if y - m < 0:
                    under = under * first["gy"]
                if y + m > size_y - 1:
                    over = over * last["gy"]
                total += stencil[m] * (under + over)
            z_part = z_term[GROUP * y : GROUP * (y + 1)]
            total += z_part[:, :128] + z_part[:, 128:]
            back_part = jnp.dot(
                coef, scatter_op[x * size_y + y], preferred_element_type=F32
            )
            total += back_part[:GROUP] + back_part[GROUP:]
            before = field[back, g, 4 + x, y].astype(F32)
            tile = (scale * total - keep * before).astype(BF16)
            field[k + 1, g, 4 + x, y] = tile
            tiles.append(tile)

        @pl.when(k < DEGREE - 1)
        def _():
            pack_z(k + 1, g, x, [field[k + 1, g, 4 + x, y].astype(F32) for y in range(size_y)])

    def slot(s, carry):
        k, g = lax.div(s, groups), lax.rem(s, groups)
        for side in range(2):
            for x in range(size_x):
                x_copy(k, g, x, side).wait_recv()
            y_copy(k, g, side).wait()
            z_copy(k, g, side).wait()

        def batch(stages):
            for age, stage in zip((3, 2, 1), stages):
                chain = s - age

                @pl.when((chain >= 0) & (chain < (DEGREE - 1) * groups))
                def _(chain=chain, stage=stage):
                    advance(chain, stage)

        def x_step(x, c):
            one_x(k, g, x)
            return c

        def pump(done, pieces):
            @pl.when((done >= 0) & (done < (DEGREE - 1) * groups))
            def _():
                for x in pieces:
                    for side in range(2):
                        x_copy(lax.div(done, groups) + 1, lax.rem(done, groups), x, side).start()

        lax.fori_loop(0, size_x // 2, x_step, 0)
        batch((4, 2, 0))
        pump(s - 1, (2, 3))
        lax.fori_loop(size_x // 2, size_x, x_step, 0)

        @pl.when(k < DEGREE - 1)
        def _():
            send_edges(k + 1, g)
            q_send[s, 0] = gather(k + 1, (g,))
            for side in range(2):
                q_copy(s, 0, side).start()

        batch((5, 3, 1))
        pump(s, (0, 1))
        return carry

    lax.fori_loop(0, DEGREE * groups, slot, 0)
    for g in range(groups):
        out_copy(g).start()

    def gram_part(x, acc):
        rows = jnp.concatenate(
            [
                jnp.concatenate([field[DEGREE, g, 4 + x, y] for y in range(size_y)], axis=1)
                for g in range(groups)
            ],
            axis=0,
        )
        nt = (((1,), (1,)), ((), ()))
        return acc + lax.dot_general(rows, rows, nt, preferred_element_type=F32)

    bands = groups * GROUP
    with jax.named_scope("gram_local"):
        gram = lax.fori_loop(0, size_x, gram_part, jnp.zeros((bands, bands), F32))
        gram = gram * (1.0 / float(size_x * size_y * 128 * span_x * span_y * span_z))
    packed = jnp.concatenate([gram[: bands // 2], gram[bands // 2 :]], axis=1)
    piece = bands // 2 // (span_y * span_z)
    for i in range(span_y * span_z):
        g_part[i // span_y, i % span_y] = packed[i * piece : (i + 1) * piece]

    def exchange(count, me, outgoing, landing, sends, recvs, place):
        def copy(other):
            return pltpu.make_async_remote_copy(
                outgoing(other), landing.at[me], sends.at[other], recvs.at[me], device_id=place(other)
            )

        def arrival(other):
            return pltpu.make_async_remote_copy(
                outgoing(other), landing.at[other], sends.at[other], recvs.at[other],
                device_id=place(other),
            )

        others = [lax.rem(me + d, count) for d in range(1, count)]
        for other in others:
            copy(other).start()
        return others, copy, arrival

    def summed(landing, count):
        total = landing[0]
        for i in range(1, count):
            total = total + landing[i]
        return total

    def finish(parts):
        others, copy, arrival = parts
        for other in others:
            arrival(other).wait_recv()
        for other in others:
            copy(other).wait_send()

    with jax.named_scope("gram_sum"):
        at_z, at_y, at_x = here["gz"], here["gy"], here["gx"]
        run = exchange(span_z, at_z, lambda o: g_part.at[o], r_z, sz.at[0], rz.at[0], lambda o: {"gz": o})
        r_z[at_z] = g_part[at_z]
        finish(run)
        s_z[...] = summed(r_z, span_z)
        run = exchange(span_y, at_y, lambda o: s_z.at[o], r_y, sy.at[0], ry.at[0], lambda o: {"gy": o})
        r_y[at_y] = s_z[at_y]
        finish(run)
        s_y[...] = summed(r_y, span_y)
        run = exchange(span_x, at_x, lambda o: s_y, r_x, sx, rx, lambda o: {"gx": o})
        r_x[at_x] = s_y[...]
        finish(run)
        g_all[at_z, at_y] = summed(r_x, span_x)
        run = exchange(span_y, at_y, lambda o: g_all.at[at_z, at_y], g_all.at[at_z], sy.at[1], ry.at[1], lambda o: {"gy": o})
        finish(run)
        run = exchange(span_z, at_z, lambda o: g_all.at[at_z], g_all, sz.at[1], rz.at[1], lambda o: {"gz": o})
        finish(run)
        for i in range(span_y * span_z):
            line = g_all[i // span_y, i % span_y]
            gram_ref[pl.ds(i * piece, piece), :] = line[:, :bands]
            gram_ref[pl.ds(bands // 2 + i * piece, piece), :] = pltpu.roll(line, bands, 1)[:, :bands]

    def close(i, c):
        k, g = lax.div(i, groups), lax.rem(i, groups)
        for side in range(2):
            for x in range(size_x):
                x_copy(k, g, x, side).wait_send()
        return c

    with jax.named_scope("close"):
        lax.fori_loop(0, DEGREE * groups, close, 0)
        for g in range(groups):
            out_copy(g).wait()


def z_weights(size_z):
    coef = [-0.5 * c / FILTER_HALF for c in STENCIL]
    whole = np.zeros((2 * size_z, size_z), np.float32)
    for z in range(size_z):
        for m in range(1, 5):
            for source in (z - m, z + m):
                if source < 0:
                    at = size_z + 4 + source
                elif source >= size_z:
                    at = size_z + 4 + source - size_z
                else:
                    at = source
                whole[at, z] = coef[m]
    high = whole.astype(ml_dtypes.bfloat16)
    low = (whole - high.astype(np.float32)).astype(ml_dtypes.bfloat16)
    return np.concatenate([high, low], axis=1)


def shards(bands, potential, coupling, proj_atom, proj_cell, proj_value):
    count, size_x, size_y, size_z = bands.shape
    entries = proj_atom.shape[1]
    groups = count // GROUP
    chains = (DEGREE - 1) * groups
    grouped = bands.reshape(groups, GROUP, size_x, size_y, size_z).transpose(0, 2, 3, 1, 4)
    vmem = pl.BlockSpec(memory_space=pltpu.VMEM)
    anywhere = pl.BlockSpec(memory_space=pl.ANY)
    dma = pltpu.SemaphoreType.DMA
    span_x, span_y, span_z = SPAN["gx"], SPAN["gy"], SPAN["gz"]
    rows = 8 * groups
    piece = count // 2 // (span_y * span_z)
    out, gram = pl.pallas_call(
        kernel,
        out_shape=(
            jax.ShapeDtypeStruct(grouped.shape, BF16),
            jax.ShapeDtypeStruct((count, count), F32),
        ),
        in_specs=[anywhere] + [vmem] * 6,
        out_specs=(anywhere, vmem),
        scratch_shapes=[
            pltpu.VMEM((DEGREE + 1, groups, 12, size_y, GROUP, size_z), BF16),
            pltpu.VMEM((DEGREE, groups, 2, size_x, 4, GROUP, size_z), BF16),
            pltpu.VMEM((DEGREE, groups, size_x, GROUP, size_z), BF16),
            pltpu.VMEM((DEGREE, groups, 2, size_x, GROUP, size_z), BF16),
            pltpu.VMEM((size_x, size_y * size_z, entries), BF16),
            pltpu.VMEM((size_x * size_y, entries, size_z), BF16),
            pltpu.VMEM((entries, 2 * KEYS), BF16),
            pltpu.VMEM((2 * KEYS, entries), BF16),
            pltpu.VMEM((DEGREE, groups, 2 * GROUP, entries), BF16),
            pltpu.VMEM((8, 128), F32),
            pltpu.VMEM((size_x, size_y, size_z), F32),
            pltpu.VMEM((chains, 6, 8, 128), F32),
            pltpu.VMEM((chains, 6, 2, 8, 128), F32),
            pltpu.VMEM((6, rows, 128), F32),
            pltpu.VMEM((6, 2, rows, 128), F32),
            pltpu.VMEM((span_z, span_y, piece, 128), F32),
            pltpu.VMEM((span_z, span_y, piece, 128), F32),
            pltpu.VMEM((span_y, piece, 128), F32),
            pltpu.VMEM((span_y, piece, 128), F32),
            pltpu.VMEM((piece, 128), F32),
            pltpu.VMEM((span_x, piece, 128), F32),
            pltpu.VMEM((span_z, span_y, piece, 128), F32),
            dma((groups,)),
            dma((groups,)),
            dma((DEGREE, groups, size_x, 2)),
            dma((DEGREE, groups, size_x, 2)),
            dma((DEGREE, groups, 2)),
            dma((DEGREE, groups, 2)),
            dma((DEGREE, groups, 2)),
            dma((DEGREE, groups, 2)),
            dma((chains, 6, 2)),
            dma((chains, 6, 2)),
            dma((6, 2)),
            dma((6, 2)),
            dma((2, span_z)),
            dma((2, span_z)),
            dma((2, span_y)),
            dma((2, span_y)),
            dma((span_x,)),
            dma((span_x,)),
        ],
        compiler_params=pltpu.CompilerParams(
            collective_id=0, has_side_effects=True, vmem_limit_bytes=48 * 1024 * 1024
        ),
    )(
        grouped,
        potential,
        coupling.reshape(-1, 128),
        proj_atom,
        proj_cell,
        proj_value,
        jnp.asarray(z_weights(size_z)),
    )
    filtered = out.transpose(0, 3, 1, 2, 4).reshape(bands.shape)
    return filtered, gram


def solution(mesh):
    SPAN.update(mesh.shape)
    in_specs = (
        P(None, "gx", "gy", "gz"),
        P("gx", "gy", "gz"),
        P(),
        P(("gx", "gy", "gz"), None),
        P(("gx", "gy", "gz"), None),
        P(("gx", "gy", "gz"), None),
    )
    out_specs = (P(None, "gx", "gy", "gz"), P())
    return jax.shard_map(shards, mesh=mesh, in_specs=in_specs, out_specs=out_specs, check_vma=False)
```

time: 631 us -> 161 us (0.26); the launches traced: 620 us -> 161 us
  starting transfers between devices: 177 us -> 0 us
  blocking collectives: 168 us -> 0 us
  Pallas kernels: 0 us -> 156 us
  other arithmetic: 107 us -> 0 us
  local copies, waits for them, and re-layouts: 104 us -> 4.49 us
  waiting for transfers between devices: 61.4 us -> 0 us
    ppermute x54 -> x0, starting transfers between devices: 177 us -> none  [the longest x27 136 us: with_halo(): lax.ppermute(lax.slice_in_dim(block, block.shape[dim] - width, None, axis...]
    psum x1 -> x0, blocking collectives: 168 us -> none  [shards(): gram = lax.psum(local_gram, ('gx', 'gy', 'gz')) / float(cells_dev * devices)]
    pallas_call x0 -> x1, Pallas kernels: none -> 156 us  [shards(): pl.pallas_call(kernel, out_shape=(jax.ShapeDtypeStruct(grouped.shape, BF1...]
    ppermute x54 -> x0, waiting for transfers between devices: 61.4 us -> none  [the longest x27 31.4 us: with_halo(): lax.ppermute(lax.slice_in_dim(block, 0, width, axis=dim), axis, backward)]
    convert_element_type x3 -> x0, other arithmetic: 56.3 us -> none  [the longest x2 32.6 us: shards(): current = following.astype(jnp.bfloat16)]
    slice x22 -> x0, local copies, waits for them, and re-layouts: 47.6 us -> none  [the longest x13 35 us: with_halo(): lax.slice_in_dim(block, 0, width, axis=dim)]
    ppermute x6 -> x0, local copies, waits for them, and re-layouts: 26.8 us -> none  [the longest x3 13.4 us: with_halo(): lax.ppermute(lax.slice_in_dim(block, 0, width, axis=dim), axis, backward)]
    scatter-add x6 -> x0, other arithmetic: 24.1 us -> none  [the longest x3 14.3 us: projector(): return jnp.zeros_like(flat).at[:, cells].add((back * values[:, None]).T)]
  transfers between devices with their start and end apart: 54 -> 0, of which waited for: 19 -> 0; matrix products, arithmetic and copies ran while one was open for 16% -> 0% of each run, Pallas kernels for 0% -> 0%
where the time goes in v1:
time: 161 us
  Pallas kernels  156 us (97%)
  local copies, waits for them, and re-layouts  4.49 us (3%)
    pallas_call x1, Pallas kernels, shards(): pl.pallas_call(kernel, out_shape=(jax.ShapeDtypeStruct(grouped.shape, BF1...  156 us

profile of v1, /device:TPU:1, one launch (start us, length us, event | category | flops | bytes accessed | tf_op | source)
XLA Modules:
  0.0 161.0 jit_solution(10812159252445270287)
XLA Ops:
  0.6 0.0 copy-start
  0.6 0.0 copy-start.1
  0.7 0.0 copy-start.2
  0.7 0.0 copy-start.4
  0.7 0.0 copy-start.5
  0.7 2.0 %copy.12 = bf16[4,16,4,16,128]{4,1,3,2,0:T(8,128)(2,1)S(1)} copy(bf16[4,16,4,16,128]{4,3,2,1,0:T(8,128)(2,1)} %bitcast.10) | data formatting | bytes 2097152 | tf_op jit(solution)/shard_map/reshape | solution.py:482
  2.7 0.0 copy-start.3
  2.7 0.0 copy-done
  2.7 0.0 copy-done.1
  2.7 0.0 copy-done.2
  2.7 0.0 copy-done.4
  2.7 0.0 copy-done.5
  2.7 0.6 copy-done.3
  3.3 155.8 %shard_map.86 = (bf16[4,4,16,16,128]{4,3,2,1,0:T(8,128)(2,1)S(1)}, f32[64,64]{1,0:T(8,128)S(1)}) custom-call(bf16[4,4,16,16,128]{4,3,2,1,0:T(8,128)(2,1)S(1)} %bitcast.7, f32[4,16,128]{2,1,0:T(8,128)S(1)} %copy-done.1, f32[16,128]{1,0:T(8,128)S(1)} %bitcast.9, s32[1,256]{1,0:T(1,128)S(1)} %copy-done.3, s32[1,256]{1,0:T(1,128)S(1)} %copy-done.4, ...), custom_call_target="tpu_custom_call" | custom-call | tf_op jit(solution)/shard_map/pallas_call | solution.py:489
  159.2 1.2 copy.10
  160.4 0.6 copy.14
Async XLA Ops:
  0.6 2.0 %copy-start = (bf16[256,256]{1,0:T(8,128)(2,1)S(1)}, bf16[256,256]{1,0:T(8,128)(2,1)}, u32[]{:S(2)}) copy-start(bf16[256,256]{1,0:T(8,128)(2,1)} %constant.2.clone.wz_ref) | copy-start | bytes 393220
  0.6 2.0 %copy-start.1 = (f32[4,16,128]{2,1,0:T(8,128)S(1)}, f32[4,16,128]{2,1,0:T(8,128)}, u32[]{:S(2)}) copy-start(f32[4,16,128]{2,1,0:T(8,128)} %pot_ref.1) | copy-start | bytes 98308
  0.7 2.0 %copy-start.2 = (f32[2048]{0:T(1024)S(1)}, f32[2048]{0:T(1024)}, u32[]{:S(2)}) copy-start(f32[2048]{0:T(1024)} %param.9) | copy-start | bytes 24580
  0.7 2.0 %copy-start.4 = (s32[1,256]{1,0:T(1,128)S(1)}, s32[1,256]{1,0:T(1,128)}, u32[]{:S(2)}) copy-start(s32[1,256]{1,0:T(1,128)} %cell_ref.1) | copy-start | bytes 3076
  0.7 2.0 %copy-start.5 = (f32[1,256]{1,0:T(1,128)S(1)}, f32[1,256]{1,0:T(1,128)}, u32[]{:S(2)}) copy-start(f32[1,256]{1,0:T(1,128)} %val_ref.1) | copy-start | bytes 3076
  2.7 0.7 copy-start.3

commit v2 on v1

--- a/solution.py
+++ b/solution.py
@@ -16,15 +16,20 @@
 GROUP = 16
 KEYS = 64
 SPAN = {}
-STAGES = (("gz", 2), ("gy", 6), ("gx", 18), ("gx", 18), ("gy", 6), ("gz", 2))
+PLANE = [(dy, dz) for dy in (-1, 0, 1) for dz in (-1, 0, 1) if dy or dz]
+ACROSS = [({"gy": dy, "gz": dz}, 6 * dy + 2 * dz) for dy, dz in PLANE]
+ALONG = [({"gx": 1}, 18), ({"gx": -1}, -18)]
+STAGES = (ACROSS, ALONG, ALONG, ACROSS)
 OWN_LANE = 26
 F32 = jnp.float32
 BF16 = jnp.bfloat16
 
 
-def beside(axis, offset):
-    n = SPAN[axis]
-    return {axis: lax.rem(lax.axis_index(axis) + offset + n, n)}
+def beside(offsets):
+    return {
+        axis: lax.rem(lax.axis_index(axis) + d + SPAN[axis], SPAN[axis])
+        for axis, d in offsets.items()
+    }
 
 
 def split(value):
@@ -35,11 +40,11 @@
 def kernel(
     y0_ref, pot_ref, coup_ref, atom_ref, cell_ref, val_ref, wz_ref,
     out_ref, gram_ref,
-    field, y_halo, z_pack, z_halo, gather_op, scatter_op, key_in, key_out, table, coup_row, potq,
+    field, y_halo, z_pack, z_halo, gather_op, scatter_op, key_in, key_out, table, coup_all, coup_row, potq,
     q_send, q_recv, q0_send, q0_recv,
     g_part, r_z, s_z, r_y, s_y, r_x, g_all,
     load_sem, out_sem, x_ss, x_rs, y_ss, y_rs, z_ss, z_rs, q_ss, q_rs, q0_ss, q0_rs,
-    sz, rz, sy, ry, sx, rx,
+    sz, rz, sy, ry, sx, rx, token,
 ):
     groups, size_x, size_y = field.shape[1], 4, field.shape[3]
     span_x, span_y, span_z = SPAN["gx"], SPAN["gy"], SPAN["gz"]
@@ -55,13 +60,13 @@
             field.at[DEGREE, g, pl.ds(4, 4)], out_ref.at[g], out_sem.at[g]
         )
 
-    def x_copy(k, g, x, side):
+    def x_copy(k, g, half, side):
         return pltpu.make_async_remote_copy(
-            field.at[k, g, 4 + x],
-            field.at[k, g, x if side == 0 else 8 + x],
-            x_ss.at[k, g, x, side],
-            x_rs.at[k, g, x, side],
-            device_id=beside("gx", 1 - 2 * side),
+            field.at[k, g, pl.ds(4 + 2 * half, 2)],
+            field.at[k, g, pl.ds(2 * half + 8 * side, 2)],
+            x_ss.at[k, g, half, side],
+            x_rs.at[k, g, half, side],
+            device_id=beside({"gx": 1 - 2 * side}),
         )
 
     def y_copy(k, g, side):
@@ -71,7 +76,7 @@
             y_halo.at[k, g, side],
             y_ss.at[k, g, side],
             y_rs.at[k, g, side],
-            device_id=beside("gy", 1 - 2 * side),
+            device_id=beside({"gy": 1 - 2 * side}),
         )
 
     def z_copy(k, g, side):
@@ -80,44 +85,53 @@
             z_halo.at[k, g, side],
             z_ss.at[k, g, side],
             z_rs.at[k, g, side],
-            device_id=beside("gz", 1 - 2 * side),
+            device_id=beside({"gz": 1 - 2 * side}),
         )
 
-    def q_copy(chain, stage, side):
-        return pltpu.make_async_remote_copy(
-            q_send.at[chain, stage],
-            q_recv.at[chain, stage, side],
-            q_ss.at[chain, stage, side],
-            q_rs.at[chain, stage, side],
-            device_id=beside(STAGES[stage][0], 1 - 2 * side),
-        )
-
-    def q0_copy(stage, side):
-        return pltpu.make_async_remote_copy(
-            q0_send.at[stage],
-            q0_recv.at[stage, side],
-            q0_ss.at[stage, side],
-            q0_rs.at[stage, side],
-            device_id=beside(STAGES[stage][0], 1 - 2 * side),
-        )
+    def q_copies(chain, stage):
+        return [
+            pltpu.make_async_remote_copy(
+                q_send.at[chain, stage],
+                q_recv.at[chain, stage, i],
+                q_ss.at[chain, stage, i],
+                q_rs.at[chain, stage, i],
+                device_id=beside(offsets),
+            )
+            for i, (offsets, _) in enumerate(STAGES[stage])
+        ]
+
+    def q0_copies(stage):
+        return [
+            pltpu.make_async_remote_copy(
+                q0_send.at[stage],
+                q0_recv.at[stage, i],
+                q0_ss.at[stage, i],
+                q0_rs.at[stage, i],
+                device_id=beside(offsets),
+            )
+            for i, (offsets, _) in enumerate(STAGES[stage])
+        ]
+
+    def start(copies):
+        for copy in copies:
+            copy.start()
+
+    def token_send():
+        for side in range(2):
+            pl.semaphore_signal(token.at[side], 1, device_id=beside({"gx": 1 - 2 * side}))
+
+    def token_wait():
+        for side in range(2):
+            pl.semaphore_wait(token.at[side], 1)
 
     for g in range(groups):
         load_copy(g).start()
+    coup_copy = pltpu.make_async_copy(coup_ref, coup_all, load_sem.at[groups])
+    coup_copy.start()
     barrier = pltpu.get_barrier_semaphore()
-    partners = [(a, d) for a in ("gx", "gy", "gz") for d in (1, -1)]
-    greeted = []
-    for axis, offset in partners:
-        greeted.append(beside(axis, offset))
-    for d in range(2, span_z - 1):
-        greeted.append(beside("gz", d))
-    for d in range(2, span_y - 1):
-        greeted.append(beside("gy", d))
-    for d in range(2, span_x - 1):
-        greeted.append(beside("gx", d))
-    with jax.named_scope("entry"):
-        for device in greeted:
-            pl.semaphore_signal(barrier, 1, device_id=device)
-        pl.semaphore_wait(barrier, len(greeted))
+    greeted = [beside(offsets) for offsets, _ in ALONG + ACROSS]
+    for device in greeted:
+        pl.semaphore_signal(barrier, 1, device_id=device)
 
     lane = lax.broadcasted_iota(jnp.int32, (GROUP, 128), 1)
     low_half = lane < KEYS
@@ -146,7 +160,7 @@
             return acc + jnp.dot(row, gather_op[x], preferred_element_type=F32)
 
         none = jnp.zeros((GROUP * len(chosen), val_ref.shape[1]), F32)
-        picked = lax.fori_loop(0, size_x, one, none)
+        picked = lax.fori_loop(0, size_x, one, none, unroll=size_x)
         high, low = split(picked * val_ref[...])
         both = jnp.dot(high, key_in[...], preferred_element_type=F32)
         both = both + jnp.dot(low, key_in[...], preferred_element_type=F32)
@@ -155,25 +169,15 @@
             [jnp.where(low_half[:8], part[:8], part[8:]) for part in parts], axis=0
         )
 
-    def first_pump(pieces):
+    def pump(k, pieces):
         for i in pieces:
             for side in range(2):
-                x_copy(0, i // size_x, i % size_x, side).start()
-
-    for g in range(groups):
-        load_copy(g).wait()
-        if g < 2:
-            first_pump(range(size_x * g, size_x * (g + 1)))
+                x_copy(k, i // 2, i % 2, side).start()
 
     def first_pack(i, carry):
         g, x = lax.div(i, size_x), lax.rem(i, size_x)
         pack_z(0, g, x, [field[0, g, 4 + x, y].astype(F32) for y in range(size_y)])
         return carry
-
-    with jax.named_scope("first_pack"):
-        lax.fori_loop(0, groups * size_x, first_pack, 0)
-        for g in range(groups):
-            send_edges(0, g)
 
     atoms = atom_ref[...]
     bits_a, bits_y, bits_z = (n.bit_length() - 1 for n in (A_DEV, span_y, span_z))
@@ -198,14 +202,12 @@
         hot = jnp.where(z_rows + r * 128 == cells, 1.0, 0.0).astype(BF16)
         gather_op[x, pl.ds(pl.multiple_of(y * 128, 128), 128)] = hot
         hot = jnp.where(z_lanes + r * 128 == cell_rows, 1.0, 0.0).astype(BF16)
-        scatter_op[r] = hot
+        scatter_op[lax.div(r, 2), :, pl.ds(pl.multiple_of(lax.rem(r, 2) * 128, 128), 128)] = hot
         return carry
 
-    with jax.named_scope("build"):
-        lax.fori_loop(0, size_x * size_y, build, 0)
-
     linear = (here["gx"] * SPAN["gy"] + here["gy"]) * SPAN["gz"] + here["gz"]
-    row = coup_ref[pl.ds(lax.div(linear * A_DEV, 128), 1)]
+    coup_copy.wait()
+    row = coup_all[pl.ds(lax.div(linear * A_DEV, 128), 1)]
     at = lax.rem(linear * A_DEV, 128)
     row = jnp.broadcast_to(row, (8, 128))
     lane8 = lane[:8]
@@ -218,15 +220,29 @@
         coup_row[...] = part if half == 0 else coup_row[...] + part
     potq[...] = (pot_ref[...] - (FILTER_CENTRE + 1.5 * STENCIL[0])) / FILTER_HALF
 
-    def combine(stage, own, from_low, from_high):
-        shift = STAGES[stage][1]
-        if stage < 3:
-            total = own + pltpu.roll(from_low, 128 - shift, 1) + pltpu.roll(from_high, shift, 1)
-            if stage == 2:
-                scale = coup_row[...]
-                total = total * jnp.concatenate([scale] * (own.shape[0] // 8), axis=0)
-            return total
-        return own + pltpu.roll(from_low, 128 - shift, 1) + pltpu.roll(from_high, shift, 1)
+    pl.semaphore_wait(barrier, len(greeted))
+    token_send()
+
+    def pump(k, pieces):
+        for i in pieces:
+            for side in range(2):
+                x_copy(k, i // 2, i % 2, side).start()
+
+    for g in range(groups):
+        load_copy(g).wait()
+        if g == 0:
+            pump(0, (0, 1))
+
+    with jax.named_scope("build"):
+        lax.fori_loop(0, size_x * size_y, build, 0)
+
+    def combine(stage, own, arrived):
+        total = own
+        for (_, shift), part in zip(STAGES[stage], arrived):
+            total = total + pltpu.roll(part, (128 - shift) % 128, 1)
+        if stage == 1:
+            total = total * jnp.concatenate([coup_row[...]] * (own.shape[0] // 8), axis=0)
+        return total
 
     def write_table(k, g, packed):
         turned = pltpu.roll(packed, KEYS, 1)
@@ -241,31 +257,38 @@
         table[k, g] = jnp.concatenate([high, back - high], axis=0).astype(BF16)
 
     def advance(chain, stage):
-        for side in range(2):
-            q_copy(chain, stage, side).wait()
-        result = combine(
-            stage, q_send[chain, stage], q_recv[chain, stage, 0], q_recv[chain, stage, 1]
-        )
-        if stage < 5:
+        for copy in q_copies(chain, stage):
+            copy.wait_recv()
+        arrived = [q_recv[chain, stage, i] for i in range(len(STAGES[stage]))]
+        result = combine(stage, q_send[chain, stage], arrived)
+        if stage < 3:
             q_send[chain, stage + 1] = result
-            for side in range(2):
-                q_copy(chain, stage + 1, side).start()
+            start(q_copies(chain, stage + 1))
         else:
-            write_table(1 + lax.div(chain, groups), lax.rem(chain, groups), result)
+            k, half = 1 + lax.div(chain, 2), lax.rem(chain, 2)
+            for i in range(2):
+                write_table(k, 2 * half + i, result[8 * i : 8 * i + 8])
 
     with jax.named_scope("first_exchange"):
         q0_send[0] = gather(0, range(groups))
-        for stage in range(6):
-            for side in range(2):
-                q0_copy(stage, side).start()
+        for stage in range(4):
+            start(q0_copies(stage))
+            if stage == 0:
+                pump(0, (2,))
+                lax.fori_loop(0, groups * size_x, first_pack, 0, unroll=2)
+                for g in range(groups):
+                    send_edges(0, g)
+            if stage == 1:
+                pump(0, (3,))
             if stage == 2:
-                first_pump(range(2 * size_x, 2 * size_x + 2))
-            if stage == 3:
-                first_pump(range(2 * size_x + 2, groups * size_x))
-            for side in range(2):
-                q0_copy(stage, side).wait()
-            result = combine(stage, q0_send[stage], q0_recv[stage, 0], q0_recv[stage, 1])
-            if stage < 5:
+                pump(0, range(4, 8))
+            token_wait()
+            token_send()
+            for copy in q0_copies(stage):
+                copy.wait_recv()
+            arrived = [q0_recv[stage, i] for i in range(len(STAGES[stage]))]
+            result = combine(stage, q0_send[stage], arrived)
+            if stage < 3:
                 q0_send[stage + 1] = result
             else:
                 for g in range(groups):
@@ -297,76 +320,113 @@
             c_high.append(jnp.where(x + m <= 3, 1.0, last["gx"]) * stencil[m])
         tiles = []
         coef = table[k, g]
+        for pair in range(size_y // 2):
+            back_part = jnp.dot(
+                coef, scatter_op[x * (size_y // 2) + pair], preferred_element_type=F32
+            )
+            for i in range(2):
+                y = 2 * pair + i
+                total = ownf[y] * potq[x, pl.ds(y, 1)]
+                for m in range(1, 5):
+                    total += c_low[m - 1] * field[k, g, 4 + x - m, y].astype(F32)
+                    total += c_high[m - 1] * field[k, g, 4 + x + m, y].astype(F32)
+                    under, over = line[4 + y - m], line[4 + y + m]
+                    if y - m < 0:
+                        under = under * first["gy"]
+                    if y + m > size_y - 1:
+                        over = over * last["gy"]
+                    total += stencil[m] * (under + over)
+                z_part = z_term[GROUP * y : GROUP * (y + 1)]
+                total += z_part[:, :128] + z_part[:, 128:]
+                mine = back_part[:, 128 * i : 128 * (i + 1)]
+                total += mine[:GROUP] + mine[GROUP:]
+                before = field[back, g, 4 + x, y].astype(F32)
+                tiles.append((scale * total - keep * before).astype(BF16))
         for y in range(size_y):
-            total = ownf[y] * potq[x, pl.ds(y, 1)]
-            for m in range(1, 5):
-                total += c_low[m - 1] * field[k, g, 4 + x - m, y].astype(F32)
-                total += c_high[m - 1] * field[k, g, 4 + x + m, y].astype(F32)
-                under, over = line[4 + y - m], line[4 + y + m]
-                if y - m < 0:
-                    under = under * first["gy"]
-                if y + m > size_y - 1:
-                    over = over * last["gy"]
-                total += stencil[m] * (under + over)
-            z_part = z_term[GROUP * y : GROUP * (y + 1)]
-            total += z_part[:, :128] + z_part[:, 128:]
-            back_part = jnp.dot(
-                coef, scatter_op[x * size_y + y], preferred_element_type=F32
-            )
-            total += back_part[:GROUP] + back_part[GROUP:]
-            before = field[back, g, 4 + x, y].astype(F32)
-            tile = (scale * total - keep * before).astype(BF16)
-            field[k + 1, g, 4 + x, y] = tile
-            tiles.append(tile)
-
-        @pl.when(k < DEGREE - 1)
-        def _():
-            pack_z(k + 1, g, x, [field[k + 1, g, 4 + x, y].astype(F32) for y in range(size_y)])
-
-    def slot(s, carry):
-        k, g = lax.div(s, groups), lax.rem(s, groups)
+            field[k + 1, g, 4 + x, y] = tiles[y]
+        pack_z(k + 1, g, x, [tile.astype(F32) for tile in tiles])
+
+    def finish_group(k, g):
         for side in range(2):
-            for x in range(size_x):
-                x_copy(k, g, x, side).wait_recv()
+            for half in range(2):
+                x_copy(k, g, half, side).wait_recv()
             y_copy(k, g, side).wait()
             z_copy(k, g, side).wait()
-
-        def batch(stages):
-            for age, stage in zip((3, 2, 1), stages):
-                chain = s - age
-
-                @pl.when((chain >= 0) & (chain < (DEGREE - 1) * groups))
-                def _(chain=chain, stage=stage):
-                    advance(chain, stage)
 
         def x_step(x, c):
             one_x(k, g, x)
             return c
 
-        def pump(done, pieces):
-            @pl.when((done >= 0) & (done < (DEGREE - 1) * groups))
-            def _():
-                for x in pieces:
-                    for side in range(2):
-                        x_copy(lax.div(done, groups) + 1, lax.rem(done, groups), x, side).start()
-
-        lax.fori_loop(0, size_x // 2, x_step, 0)
-        batch((4, 2, 0))
-        pump(s - 1, (2, 3))
-        lax.fori_loop(size_x // 2, size_x, x_step, 0)
-
-        @pl.when(k < DEGREE - 1)
+        lax.fori_loop(0, size_x, x_step, 0, unroll=size_x)
+
+    def round_of(k, carry):
+        more = k < DEGREE - 1
+
+        def begin(half):
+            chain = 2 * k + half
+            q_send[chain, 0] = gather(k + 1, (2 * half, 2 * half + 1))
+            start(q_copies(chain, 0))
+
+        @pl.when(k > 0)
         def _():
-            send_edges(k + 1, g)
-            q_send[s, 0] = gather(k + 1, (g,))
-            for side in range(2):
-                q_copy(s, 0, side).start()
-
-        batch((5, 3, 1))
-        pump(s, (0, 1))
+            advance(2 * k - 1, 1)
+            pump(k, (7,))
+
+        token_wait()
+        token_send()
+        finish_group(k, 0)
+
+        @pl.when(more)
+        def _():
+            pump(k + 1, (0, 1))
+            send_edges(k + 1, 0)
+
+        @pl.when(k > 0)
+        def _():
+            advance(2 * k - 1, 2)
+
+        token_wait()
+        token_send()
+        finish_group(k, 1)
+
+        @pl.when(more)
+        def _():
+            begin(0)
+            pump(k + 1, (2,))
+            send_edges(k + 1, 1)
+
+        @pl.when(k > 0)
+        def _():
+            advance(2 * k - 1, 3)
+
+        finish_group(k, 2)
+
+        @pl.when(more)
+        def _():
+            advance(2 * k, 0)
+            pump(k + 1, (3,))
+            send_edges(k + 1, 2)
+
+        token_wait()
+        token_send()
+        finish_group(k, 3)
+
+        @pl.when(more)
+        def _():
+            advance(2 * k, 1)
+            pump(k + 1, (4,))
+            send_edges(k + 1, 3)
+            begin(1)
+            token_wait()
+            token_send()
+            advance(2 * k, 2)
+            advance(2 * k + 1, 0)
+            pump(k + 1, (5, 6))
+            advance(2 * k, 3)
+
         return carry
 
-    lax.fori_loop(0, DEGREE * groups, slot, 0)
+    lax.fori_loop(0, DEGREE, round_of, 0)
     for g in range(groups):
         out_copy(g).start()
 
@@ -383,7 +443,7 @@
 
     bands = groups * GROUP
     with jax.named_scope("gram_local"):
-        gram = lax.fori_loop(0, size_x, gram_part, jnp.zeros((bands, bands), F32))
+        gram = lax.fori_loop(0, size_x, gram_part, jnp.zeros((bands, bands), F32), unroll=size_x)
         gram = gram * (1.0 / float(size_x * size_y * 128 * span_x * span_y * span_z))
     packed = jnp.concatenate([gram[: bands // 2], gram[bands // 2 :]], axis=1)
     piece = bands // 2 // (span_y * span_z)
@@ -402,7 +462,8 @@
                 device_id=place(other),
             )
 
-        others = [lax.rem(me + d, count) for d in range(1, count)]
+        far_first = sorted(range(1, count), key=lambda d: -min(d, count - d))
+        others = [lax.rem(me + d, count) for d in far_first]
         for other in others:
             copy(other).start()
         return others, copy, arrival
@@ -413,13 +474,15 @@
             total = total + landing[i]
         return total
 
+    open_sends = []
+
     def finish(parts):
         others, copy, arrival = parts
-        for other in others:
+        for other in reversed(others):
             arrival(other).wait_recv()
-        for other in others:
-            copy(other).wait_send()
-
+        open_sends.append((others, copy))
+
+    token_wait()
     with jax.named_scope("gram_sum"):
         at_z, at_y, at_x = here["gz"], here["gy"], here["gx"]
         run = exchange(span_z, at_z, lambda o: g_part.at[o], r_z, sz.at[0], rz.at[0], lambda o: {"gz": o})
@@ -446,12 +509,25 @@
     def close(i, c):
         k, g = lax.div(i, groups), lax.rem(i, groups)
         for side in range(2):
-            for x in range(size_x):
-                x_copy(k, g, x, side).wait_send()
+            for half in range(2):
+                x_copy(k, g, half, side).wait_send()
+        return c
+
+    def close_chain(chain, c):
+        for stage in range(4):
+            for copy in q_copies(chain, stage):
+                copy.wait_send()
         return c
 
     with jax.named_scope("close"):
         lax.fori_loop(0, DEGREE * groups, close, 0)
+        lax.fori_loop(0, 2 * (DEGREE - 1), close_chain, 0)
+        for stage in range(4):
+            for copy in q0_copies(stage):
+                copy.wait_send()
+        for others, copy in open_sends:
+            for other in others:
+                copy(other).wait_send()
         for g in range(groups):
             out_copy(g).wait()
 
@@ -478,7 +554,7 @@
     count, size_x, size_y, size_z = bands.shape
     entries = proj_atom.shape[1]
     groups = count // GROUP
-    chains = (DEGREE - 1) * groups
+    chains = 2 * (DEGREE - 1)
     grouped = bands.reshape(groups, GROUP, size_x, size_y, size_z).transpose(0, 2, 3, 1, 4)
     vmem = pl.BlockSpec(memory_space=pltpu.VMEM)
     anywhere = pl.BlockSpec(memory_space=pl.ANY)
@@ -492,24 +568,25 @@
             jax.ShapeDtypeStruct(grouped.shape, BF16),
             jax.ShapeDtypeStruct((count, count), F32),
         ),
-        in_specs=[anywhere] + [vmem] * 6,
+        in_specs=[anywhere, vmem, anywhere] + [vmem] * 4,
         out_specs=(anywhere, vmem),
         scratch_shapes=[
             pltpu.VMEM((DEGREE + 1, groups, 12, size_y, GROUP, size_z), BF16),
             pltpu.VMEM((DEGREE, groups, 2, size_x, 4, GROUP, size_z), BF16),
-            pltpu.VMEM((DEGREE, groups, size_x, GROUP, size_z), BF16),
+            pltpu.VMEM((DEGREE + 1, groups, size_x, GROUP, size_z), BF16),
             pltpu.VMEM((DEGREE, groups, 2, size_x, GROUP, size_z), BF16),
             pltpu.VMEM((size_x, size_y * size_z, entries), BF16),
-            pltpu.VMEM((size_x * size_y, entries, size_z), BF16),
+            pltpu.VMEM((size_x * size_y // 2, entries, 2 * size_z), BF16),
             pltpu.VMEM((entries, 2 * KEYS), BF16),
             pltpu.VMEM((2 * KEYS, entries), BF16),
             pltpu.VMEM((DEGREE, groups, 2 * GROUP, entries), BF16),
+            pltpu.VMEM((coupling.size // 128, 128), F32),
             pltpu.VMEM((8, 128), F32),
             pltpu.VMEM((size_x, size_y, size_z), F32),
-            pltpu.VMEM((chains, 6, 8, 128), F32),
-            pltpu.VMEM((chains, 6, 2, 8, 128), F32),
-            pltpu.VMEM((6, rows, 128), F32),
-            pltpu.VMEM((6, 2, rows, 128), F32),
+            pltpu.VMEM((chains, 4, rows // 2, 128), F32),
+            pltpu.VMEM((chains, 4, 8, rows // 2, 128), F32),
+            pltpu.VMEM((4, rows, 128), F32),
+            pltpu.VMEM((4, 8, rows, 128), F32),
             pltpu.VMEM((span_z, span_y, piece, 128), F32),
             pltpu.VMEM((span_z, span_y, piece, 128), F32),
             pltpu.VMEM((span_y, piece, 128), F32),
@@ -517,24 +594,25 @@
             pltpu.VMEM((piece, 128), F32),
             pltpu.VMEM((span_x, piece, 128), F32),
             pltpu.VMEM((span_z, span_y, piece, 128), F32),
+            dma((groups + 1,)),
             dma((groups,)),
-            dma((groups,)),
-            dma((DEGREE, groups, size_x, 2)),
-            dma((DEGREE, groups, size_x, 2)),
+            dma((DEGREE, groups, 2, 2)),
+            dma((DEGREE, groups, 2, 2)),
             dma((DEGREE, groups, 2)),
             dma((DEGREE, groups, 2)),
             dma((DEGREE, groups, 2)),
             dma((DEGREE, groups, 2)),
-            dma((chains, 6, 2)),
-            dma((chains, 6, 2)),
-            dma((6, 2)),
-            dma((6, 2)),
+            dma((chains, 4, 8)),
+            dma((chains, 4, 8)),
+            dma((4, 8)),
+            dma((4, 8)),
             dma((2, span_z)),
             dma((2, span_z)),
             dma((2, span_y)),
             dma((2, span_y)),
             dma((span_x,)),
             dma((span_x,)),
+            pltpu.SemaphoreType.REGULAR((2,)),
         ],
         compiler_params=pltpu.CompilerParams(
             collective_id=0, has_side_effects=True, vmem_limit_bytes=48 * 1024 * 1024

time: 161 us -> 140 us (0.87)
  Pallas kernels: 156 us -> 135 us
    pallas_call x1, Pallas kernels: 156 us -> 135 us  [shards(): pl.pallas_call(kernel, out_shape=(jax.ShapeDtypeStruct(grouped.shape, BF1...]
where the time goes in v2:
time: 140 us
  Pallas kernels  135 us (96%)
  local copies, waits for them, and re-layouts  4.49 us (3%)
    pallas_call x1, Pallas kernels, shards(): pl.pallas_call(kernel, out_shape=(jax.ShapeDtypeStruct(grouped.shape, BF1...  135 us

profile of v2, /device:TPU:1, one launch (start us, length us, event | category | flops | bytes accessed | tf_op | source)
XLA Modules:
  0.0 140.3 jit_solution(5008107866977519529)
XLA Ops:
  0.6 0.0 copy-start
  0.6 0.0 copy-start.1
  0.7 0.0 copy-start.2
  0.7 0.0 copy-start.4
  0.7 0.0 copy-start.5
  0.7 2.0 %copy.12 = bf16[4,16,4,16,128]{4,1,3,2,0:T(8,128)(2,1)S(1)} copy(bf16[4,16,4,16,128]{4,3,2,1,0:T(8,128)(2,1)} %bitcast.10) | data formatting | bytes 2097152 | tf_op jit(solution)/shard_map/reshape | solution.py:558
  2.7 0.0 copy-start.3
  2.7 0.0 copy-done
  2.7 0.0 copy-done.1
  2.7 0.0 copy-done.2
  2.7 0.0 copy-done.4
  2.7 0.0 copy-done.5
  2.7 0.6 copy-done.3
  3.3 135.0 %shard_map.86 = (bf16[4,4,16,16,128]{4,3,2,1,0:T(8,128)(2,1)S(1)}, f32[64,64]{1,0:T(8,128)S(1)}) custom-call(bf16[4,4,16,16,128]{4,3,2,1,0:T(8,128)(2,1)S(1)} %bitcast.7, f32[4,16,128]{2,1,0:T(8,128)S(1)} %copy-done.1, f32[16,128]{1,0:T(8,128)S(1)} %bitcast.9, s32[1,256]{1,0:T(1,128)S(1)} %copy-done.3, s32[1,256]{1,0:T(1,128)S(1)} %copy-done.4, ...), custom_call_target="tpu_custom_call" | custom-call | tf_op jit(solution)/shard_map/pallas_call | solution.py:565
  138.4 1.2 copy.10
  139.6 0.6 copy.14
Async XLA Ops:
  0.6 2.0 %copy-start = (bf16[256,256]{1,0:T(8,128)(2,1)S(1)}, bf16[256,256]{1,0:T(8,128)(2,1)}, u32[]{:S(2)}) copy-start(bf16[256,256]{1,0:T(8,128)(2,1)} %constant.2.clone.wz_ref) | copy-start | bytes 393220
  0.6 2.0 %copy-start.1 = (f32[4,16,128]{2,1,0:T(8,128)S(1)}, f32[4,16,128]{2,1,0:T(8,128)}, u32[]{:S(2)}) copy-start(f32[4,16,128]{2,1,0:T(8,128)} %pot_ref.1) | copy-start | bytes 98308
  0.7 2.0 %copy-start.2 = (f32[2048]{0:T(1024)S(1)}, f32[2048]{0:T(1024)}, u32[]{:S(2)}) copy-start(f32[2048]{0:T(1024)} %param.9) | copy-start | bytes 24580
  0.7 2.0 %copy-start.4 = (s32[1,256]{1,0:T(1,128)S(1)}, s32[1,256]{1,0:T(1,128)}, u32[]{:S(2)}) copy-start(s32[1,256]{1,0:T(1,128)} %cell_ref.1) | copy-start | bytes 3076
  0.7 2.0 %copy-start.5 = (f32[1,256]{1,0:T(1,128)S(1)}, f32[1,256]{1,0:T(1,128)}, u32[]{:S(2)}) copy-start(f32[1,256]{1,0:T(1,128)} %val_ref.1) | copy-start | bytes 3076
  2.7 0.7 copy-start.3

commit v3 on v2

--- a/solution.py
+++ b/solution.py
@@ -245,16 +245,28 @@
         return total
 
     def write_table(k, g, packed):
+        count = packed.shape[0] // 8
         turned = pltpu.roll(packed, KEYS, 1)
-        first_bands = jnp.where(low_half[:8], packed, turned)
-        other_bands = jnp.where(low_half[:8], turned, packed)
-        whole = jnp.concatenate([first_bands, other_bands], axis=0)
+        low = lax.broadcasted_iota(jnp.int32, packed.shape, 1) < KEYS
+        first_bands = jnp.where(low, packed, turned)
+        other_bands = jnp.where(low, turned, packed)
+        whole = jnp.concatenate(
+            [
+                part[8 * i : 8 * i + 8]
+                for i in range(count)
+                for part in (first_bands, other_bands)
+            ],
+            axis=0,
+        )
         high, low = split(whole)
         back = jnp.dot(high, key_out[...], preferred_element_type=F32)
         back = back + jnp.dot(low, key_out[...], preferred_element_type=F32)
         back = back * val_ref[...]
         high = back.astype(BF16).astype(F32)
-        table[k, g] = jnp.concatenate([high, back - high], axis=0).astype(BF16)
+        rest = back - high
+        for i in range(count):
+            rows = slice(GROUP * i, GROUP * (i + 1))
+            table[k, g + i] = jnp.concatenate([high[rows], rest[rows]], axis=0).astype(BF16)
 
     def advance(chain, stage):
         for copy in q_copies(chain, stage):
@@ -266,8 +278,7 @@
             start(q_copies(chain, stage + 1))
         else:
             k, half = 1 + lax.div(chain, 2), lax.rem(chain, 2)
-            for i in range(2):
-                write_table(k, 2 * half + i, result[8 * i : 8 * i + 8])
+            write_table(k, 2 * half, result)
 
     with jax.named_scope("first_exchange"):
         q0_send[0] = gather(0, range(groups))
@@ -291,8 +302,7 @@
             if stage < 3:
                 q0_send[stage + 1] = result
             else:
-                for g in range(groups):
-                    write_table(0, g, result[8 * g : 8 * g + 8])
+                write_table(0, 0, result)
 
     stencil = [-0.5 * c / FILTER_HALF for c in STENCIL]
 
@@ -367,10 +377,25 @@
             q_send[chain, 0] = gather(k + 1, (2 * half, 2 * half + 1))
             start(q_copies(chain, 0))
 
+        def pump_first(pieces):
+            @pl.when(k == 0)
+            def _():
+                pump(k + 1, pieces)
+
+        def pump_later(pieces):
+            @pl.when(k > 0)
+            def _():
+                pump(k + 1, pieces)
+
         @pl.when(k > 0)
         def _():
             advance(2 * k - 1, 1)
-            pump(k, (7,))
+
+            @pl.when(k > 1)
+            def _():
+                pump(k, (3, 4))
+
+            pump(k, (5, 6, 7))
 
         token_wait()
         token_send()
@@ -378,7 +403,7 @@
 
         @pl.when(more)
         def _():
-            pump(k + 1, (0, 1))
+            pump_first((0, 1))
             send_edges(k + 1, 0)
 
         @pl.when(k > 0)
@@ -392,7 +417,6 @@
         @pl.when(more)
         def _():
             begin(0)
-            pump(k + 1, (2,))
             send_edges(k + 1, 1)
 
         @pl.when(k > 0)
@@ -404,7 +428,8 @@
         @pl.when(more)
         def _():
             advance(2 * k, 0)
-            pump(k + 1, (3,))
+            pump_first((2,))
+            pump_later((0,))
             send_edges(k + 1, 2)
 
         token_wait()
@@ -413,15 +438,17 @@
 
         @pl.when(more)
         def _():
+            begin(1)
             advance(2 * k, 1)
-            pump(k + 1, (4,))
+            pump_first((3,))
+            pump_later((1,))
             send_edges(k + 1, 3)
-            begin(1)
             token_wait()
             token_send()
             advance(2 * k, 2)
             advance(2 * k + 1, 0)
-            pump(k + 1, (5, 6))
+            pump_first((4,))
+            pump_later((2,))
             advance(2 * k, 3)
 
         return carry

time: 140 us -> 138 us (0.986)
  Pallas kernels: 135 us -> 133 us
    pallas_call x1, Pallas kernels: 135 us -> 133 us  [shards(): pl.pallas_call(kernel, out_shape=(jax.ShapeDtypeStruct(grouped.shape, BF1...]
where the time goes in v3:
time: 138 us
  Pallas kernels  133 us (96%)
  local copies, waits for them, and re-layouts  4.49 us (3%)
    pallas_call x1, Pallas kernels, shards(): pl.pallas_call(kernel, out_shape=(jax.ShapeDtypeStruct(grouped.shape, BF1...  133 us

profile of v3, /device:TPU:1, one launch (start us, length us, event | category | flops | bytes accessed | tf_op | source)
XLA Modules:
  0.0 137.8 jit_solution(2301917106562579898)
XLA Ops:
  0.6 0.0 copy-start
  0.6 0.0 copy-start.1
  0.7 0.0 copy-start.2
  0.7 0.0 copy-start.4
  0.7 0.0 copy-start.5
  0.7 2.0 %copy.12 = bf16[4,16,4,16,128]{4,1,3,2,0:T(8,128)(2,1)S(1)} copy(bf16[4,16,4,16,128]{4,3,2,1,0:T(8,128)(2,1)} %bitcast.10) | data formatting | bytes 2097152 | tf_op jit(solution)/shard_map/reshape | solution.py:585
  2.7 0.0 copy-start.3
  2.7 0.0 copy-done
  2.7 0.0 copy-done.1
  2.7 0.0 copy-done.2
  2.7 0.0 copy-done.4
  2.7 0.0 copy-done.5
  2.7 0.6 copy-done.3
  3.3 132.6 %shard_map.86 = (bf16[4,4,16,16,128]{4,3,2,1,0:T(8,128)(2,1)S(1)}, f32[64,64]{1,0:T(8,128)S(1)}) custom-call(bf16[4,4,16,16,128]{4,3,2,1,0:T(8,128)(2,1)S(1)} %bitcast.7, f32[4,16,128]{2,1,0:T(8,128)S(1)} %copy-done.1, f32[16,128]{1,0:T(8,128)S(1)} %bitcast.9, s32[1,256]{1,0:T(1,128)S(1)} %copy-done.3, s32[1,256]{1,0:T(1,128)S(1)} %copy-done.4, ...), custom_call_target="tpu_custom_call" | custom-call | tf_op jit(solution)/shard_map/pallas_call | solution.py:592
  136.0 1.2 copy.10
  137.2 0.6 copy.14
Async XLA Ops:
  0.6 2.0 %copy-start = (bf16[256,256]{1,0:T(8,128)(2,1)S(1)}, bf16[256,256]{1,0:T(8,128)(2,1)}, u32[]{:S(2)}) copy-start(bf16[256,256]{1,0:T(8,128)(2,1)} %constant.2.clone.wz_ref) | copy-start | bytes 393220
  0.6 2.0 %copy-start.1 = (f32[4,16,128]{2,1,0:T(8,128)S(1)}, f32[4,16,128]{2,1,0:T(8,128)}, u32[]{:S(2)}) copy-start(f32[4,16,128]{2,1,0:T(8,128)} %pot_ref.1) | copy-start | bytes 98308
  0.7 2.0 %copy-start.2 = (f32[2048]{0:T(1024)S(1)}, f32[2048]{0:T(1024)}, u32[]{:S(2)}) copy-start(f32[2048]{0:T(1024)} %param.9) | copy-start | bytes 24580
  0.7 2.0 %copy-start.4 = (s32[1,256]{1,0:T(1,128)S(1)}, s32[1,256]{1,0:T(1,128)}, u32[]{:S(2)}) copy-start(s32[1,256]{1,0:T(1,128)} %cell_ref.1) | copy-start | bytes 3076
  0.7 2.0 %copy-start.5 = (f32[1,256]{1,0:T(1,128)S(1)}, f32[1,256]{1,0:T(1,128)}, u32[]{:S(2)}) copy-start(f32[1,256]{1,0:T(1,128)} %val_ref.1) | copy-start | bytes 3076
  2.7 0.7 copy-start.3
